TPU v7x, 32 devices: a whole 2x2x4 slice. The times are simulated.
32 devices in a mesh: rep: 2 (over y), seq: 4 (over z), tp: 2 (over x), pp: 2 (over core).
Axes of the slice: x: 2, y: 2, z: 4, core: 2. Of those that a mesh axis runs over, the one named last changes fastest.
Arguments:
- queries: bfloat16 [128, 32, 8192], P(('rep', 'seq'), None, ('tp', 'pp')), parts along dimension 0, may hold values from -26 to 26
- resp_kv: bfloat16 [128, 32, 8, 256], P(('rep', 'seq'), None, 'tp'), parts along dimension 0, may hold values from -4.5 to 4.5
- prompt_kv: bfloat16 [8, 2048, 8, 256], P(('rep', 'seq'), None, 'tp'), parts along dimension 0, may hold values from -4.5 to 4.5
- lengths: int32 [128], P(('rep', 'seq')), parts along dimension 0, may hold values from 8 to 32
- group_of: int32 [128], P(('rep', 'seq')), parts along dimension 0, may hold values from 0 to 3, as said below
Outputs:
- mixed: bfloat16 [128, 32, 8192], P(('rep', 'seq'), None, ('tp', 'pp')), parts along dimension 0
There are 2 independent parts, one for each index of `rep`. A program takes and returns all parts, laid end to end along the dimension named above; each array names one. Nothing has to cross between parts.
Inputs may be any that keep to these rules, and one draw needn't show every extreme that they name: `group_of`: each device of seq holds 16 responses; every prompt is answered by exactly 16 responses; at most 8 of the responses of one device answer the same prompt, and every device has a prompt with exactly 8 of its responses.
All inputs are finite; a program needn't handle non-finite values.
Results may differ from a plain program's by a relative error of at most 0.0049.
Values may be sent and summed in bfloat16 or wider, within the bound.
No kernel may reach another device: no remote copies, remote signals or barrier semaphores. Data moves between devices by JAX's collectives and lax.ppermute only.
A program may use at most 128 MiB of HBM per device.

v0:
```python
import jax
import jax.numpy as jnp
from jax import lax
from jax.sharding import PartitionSpec as P

QHEADS = 64
KVH = 8


def attend(q_rows, resp_pairs, prompt_pairs):
    head_size = resp_pairs.shape[2] // 2
    kv_count = resp_pairs.shape[1]
    row_count = q_rows.shape[0]
    per_kv = q_rows.shape[1] // (kv_count * head_size)
    score_scale = head_size ** (-0.5)
    query = q_rows.reshape(row_count, kv_count, per_kv, head_size)
    prompt_scores = (
        jnp.einsum(
            "tkgd,skd->kgts",
            query,
            prompt_pairs[:, :, :head_size],
            preferred_element_type=jnp.float32,
        )
        * score_scale
    )
    own_scores = (
        jnp.einsum(
            "tkgd,skd->kgts",
            query,
            resp_pairs[:, :, :head_size],
            preferred_element_type=jnp.float32,
        )
        * score_scale
    )
    causal = jnp.arange(row_count)[:, None] >= jnp.arange(row_count)[None, :]
    own_scores = jnp.where(causal, own_scores, -1e30)
    peak_score = jnp.maximum(jnp.max(prompt_scores, axis=-1), jnp.max(own_scores, axis=-1))
    prompt_exp = jnp.exp(prompt_scores - peak_score[..., None])
    own_exp = jnp.exp(own_scores - peak_score[..., None])
    denominator = jnp.sum(prompt_exp, axis=-1) + jnp.sum(own_exp, axis=-1)
    prompt_weights = (prompt_exp / denominator[..., None]).astype(jnp.bfloat16)
    own_weights = (own_exp / denominator[..., None]).astype(jnp.bfloat16)
    output = jnp.einsum(
        "kgts,skd->tkgd",
        prompt_weights,
        prompt_pairs[:, :, head_size:],
        preferred_element_type=jnp.float32,
    )
    output = output + jnp.einsum(
        "kgts,skd->tkgd",
        own_weights,
        resp_pairs[:, :, head_size:],
        preferred_element_type=jnp.float32,
    )
    return output.reshape(row_count, kv_count * per_kv * head_size).astype(jnp.bfloat16)


def shards(queries, resp_kv, prompt_kv, lengths, group_of):
    head_size = resp_kv.shape[3] // 2
    local_heads = queries.shape[2] // head_size
    per_kv = QHEADS // KVH
    kv_needed = max(local_heads // per_kv, 1)
    first_head = lax.axis_index("pp") * local_heads // per_kv
    own_pairs = lax.dynamic_slice_in_dim(resp_kv, first_head, kv_needed, 2)
    holders = group_of.shape[0]
    piece = lax.all_gather(prompt_kv, "seq", axis=0, tiled=True)
    count = piece.shape[0]

    def one_response(index, holding):
        local_index = group_of[index]
        inside = (local_index >= 0) & (local_index < count)

        def compute(current):
            safe_index = jnp.clip(local_index, 0, count - 1)
            whole_prompt = lax.dynamic_index_in_dim(piece, safe_index, 0, keepdims=False)
            prompt_pairs = lax.dynamic_slice_in_dim(whole_prompt, first_head, kv_needed, 1)
            q_rows = lax.dynamic_index_in_dim(queries, index, 0, keepdims=False)
            pairs_rows = lax.dynamic_index_in_dim(own_pairs, index, 0, keepdims=False)
            answer = attend(q_rows, pairs_rows, prompt_pairs)
            return lax.dynamic_update_index_in_dim(current, answer, index, 0)

        return lax.cond(inside, compute, lambda current: current, holding)

    mixed = lax.fori_loop(0, holders, one_response, jnp.zeros(queries.shape, jnp.bfloat16))
    alive_rows = jnp.arange(queries.shape[1])[None, :] < lengths[:, None]
    return jnp.where(alive_rows[:, :, None], mixed, jnp.zeros((), jnp.bfloat16))


def solution(mesh):
    placed = (
        P(("rep", "seq"), None, ("tp", "pp")),
        P(("rep", "seq"), None, "tp", None),
        P(("rep", "seq"), None, "tp", None),
        P(("rep", "seq")),
        P(("rep", "seq")),
    )
    return jax.shard_map(
        shards,
        mesh=mesh,
        in_specs=placed,
        out_specs=P(("rep", "seq"), None, ("tp", "pp")),
        check_vma=False,
    )
```

profile of v0, /device:TPU:0, one launch (start us, length us, event | category | flops | bytes accessed | tf_op | source)
XLA Modules:
  0.0 472.8 jit_solution(12542705129958407187)
XLA Ops:
  6.5 4.7 %copy.19 = bf16[1,2048,4,256]{3,1,2,0:T(8,128)(2,1)} copy(bf16[1,2048,4,256]{3,2,1,0:T(4,128)(2,1)} %param.11) | data formatting | bytes 8388608 | tf_op args[2]
  12.9 288.0 %all-gather.2.cloned.1.call-done = bf16[4,2048,4,256]{3,1,2,0:T(8,128)(2,1)} async-done(((bf16[1,2048,4,256]{3,1,2,0:T(8,128)(2,1)}), bf16[4,2048,4,256]{3,1,2,0:T(8,128)(2,1)}) %all-gather.2.cloned.1.call-update) | async-done | bytes 16777232 | tf_op jit(solution)/shard_map/all_gather | solution.py:66
  301.2 163.2 %while.16 = (s32[]{:T(128)}, bf16[16,32,2048]{2,1,0:T(8,128)(2,1)S(1)}, s32[16]{0:T(128)S(1)}, s32[]{:T(128)}, bf16[4,2048,4,256]{3,1,2,0:T(8,128)(2,1)}, /*inde...) while((s32[]{:T(128)}, ...), condition=%wide.region_7.8_spmd, body=%wide.region_0.7_spmd.sunk | while | flops 554958848 | bytes 21919124 | solution.py:84
  303.1 8.3 %conditional.2 = (bf16[16,32,2048]{2,1,0:T(8,128)(2,1)S(1)}) conditional(s32[]{:T(128)} %convert_element_type.37, bf16[16,32,2048]{2,1,0:T(8,128)(2,1)S(1)} %get-tuple-element.231, (s32[]{:T(128)}, s32[]{:T(128)}, bf16[4,2048,4,256]{3,1,2,0:T(8,128)(2,1)}, s32[]{:T(128)}, bf16[16,32,2048]{2,1,0:T(8,128)(2,1)}, ...), branch_computations={%region_1.1_spmd, %region_2.6_spmd} | conditional | flops 554958848 | bytes 21918928 | solution.py:82
  306.4 1.7 dynamic-slice_bitcast_fusion
  313.3 8.3 %conditional.2 = (bf16[16,32,2048]{2,1,0:T(8,128)(2,1)S(1)}) conditional(s32[]{:T(128)} %convert_element_type.37, bf16[16,32,2048]{2,1,0:T(8,128)(2,1)S(1)} %get-tuple-element.231, (s32[]{:T(128)}, s32[]{:T(128)}, bf16[4,2048,4,256]{3,1,2,0:T(8,128)(2,1)}, s32[]{:T(128)}, bf16[16,32,2048]{2,1,0:T(8,128)(2,1)}, ...), branch_computations={%region_1.1_spmd, %region_2.6_spmd} | conditional | flops 554958848 | bytes 21918928 | solution.py:82
  316.6 1.7 dynamic-slice_bitcast_fusion
  320.0 1.1 fusion.2
  323.5 8.3 %conditional.2 = (bf16[16,32,2048]{2,1,0:T(8,128)(2,1)S(1)}) conditional(s32[]{:T(128)} %convert_element_type.37, bf16[16,32,2048]{2,1,0:T(8,128)(2,1)S(1)} %get-tuple-element.231, (s32[]{:T(128)}, s32[]{:T(128)}, bf16[4,2048,4,256]{3,1,2,0:T(8,128)(2,1)}, s32[]{:T(128)}, bf16[16,32,2048]{2,1,0:T(8,128)(2,1)}, ...), branch_computations={%region_1.1_spmd, %region_2.6_spmd} | conditional | flops 554958848 | bytes 21918928 | solution.py:82
  326.8 1.7 dynamic-slice_bitcast_fusion
  330.2 1.1 fusion.2
  333.7 8.3 %conditional.2 = (bf16[16,32,2048]{2,1,0:T(8,128)(2,1)S(1)}) conditional(s32[]{:T(128)} %convert_element_type.37, bf16[16,32,2048]{2,1,0:T(8,128)(2,1)S(1)} %get-tuple-element.231, (s32[]{:T(128)}, s32[]{:T(128)}, bf16[4,2048,4,256]{3,1,2,0:T(8,128)(2,1)}, s32[]{:T(128)}, bf16[16,32,2048]{2,1,0:T(8,128)(2,1)}, ...), branch_computations={%region_1.1_spmd, %region_2.6_spmd} | conditional | flops 554958848 | bytes 21918928 | solution.py:82
  337.0 1.7 dynamic-slice_bitcast_fusion
  340.4 1.1 fusion.2
  343.9 8.3 %conditional.2 = (bf16[16,32,2048]{2,1,0:T(8,128)(2,1)S(1)}) conditional(s32[]{:T(128)} %convert_element_type.37, bf16[16,32,2048]{2,1,0:T(8,128)(2,1)S(1)} %get-tuple-element.231, (s32[]{:T(128)}, s32[]{:T(128)}, bf16[4,2048,4,256]{3,1,2,0:T(8,128)(2,1)}, s32[]{:T(128)}, bf16[16,32,2048]{2,1,0:T(8,128)(2,1)}, ...), branch_computations={%region_1.1_spmd, %region_2.6_spmd} | conditional | flops 554958848 | bytes 21918928 | solution.py:82
  347.2 1.7 dynamic-slice_bitcast_fusion
  350.6 1.1 fusion.2
  354.1 8.3 %conditional.2 = (bf16[16,32,2048]{2,1,0:T(8,128)(2,1)S(1)}) conditional(s32[]{:T(128)} %convert_element_type.37, bf16[16,32,2048]{2,1,0:T(8,128)(2,1)S(1)} %get-tuple-element.231, (s32[]{:T(128)}, s32[]{:T(128)}, bf16[4,2048,4,256]{3,1,2,0:T(8,128)(2,1)}, s32[]{:T(128)}, bf16[16,32,2048]{2,1,0:T(8,128)(2,1)}, ...), branch_computations={%region_1.1_spmd, %region_2.6_spmd} | conditional | flops 554958848 | bytes 21918928 | solution.py:82
  357.4 1.7 dynamic-slice_bitcast_fusion
  360.8 1.1 fusion.2
  364.3 8.3 %conditional.2 = (bf16[16,32,2048]{2,1,0:T(8,128)(2,1)S(1)}) conditional(s32[]{:T(128)} %convert_element_type.37, bf16[16,32,2048]{2,1,0:T(8,128)(2,1)S(1)} %get-tuple-element.231, (s32[]{:T(128)}, s32[]{:T(128)}, bf16[4,2048,4,256]{3,1,2,0:T(8,128)(2,1)}, s32[]{:T(128)}, bf16[16,32,2048]{2,1,0:T(8,128)(2,1)}, ...), branch_computations={%region_1.1_spmd, %region_2.6_spmd} | conditional | flops 554958848 | bytes 21918928 | solution.py:82
  367.6 1.7 dynamic-slice_bitcast_fusion
  371.0 1.1 fusion.2
  374.5 8.3 %conditional.2 = (bf16[16,32,2048]{2,1,0:T(8,128)(2,1)S(1)}) conditional(s32[]{:T(128)} %convert_element_type.37, bf16[16,32,2048]{2,1,0:T(8,128)(2,1)S(1)} %get-tuple-element.231, (s32[]{:T(128)}, s32[]{:T(128)}, bf16[4,2048,4,256]{3,1,2,0:T(8,128)(2,1)}, s32[]{:T(128)}, bf16[16,32,2048]{2,1,0:T(8,128)(2,1)}, ...), branch_computations={%region_1.1_spmd, %region_2.6_spmd} | conditional | flops 554958848 | bytes 21918928 | solution.py:82
  377.8 1.7 dynamic-slice_bitcast_fusion
  381.2 1.1 fusion.2
  384.7 8.3 %conditional.2 = (bf16[16,32,2048]{2,1,0:T(8,128)(2,1)S(1)}) conditional(s32[]{:T(128)} %convert_element_type.37, bf16[16,32,2048]{2,1,0:T(8,128)(2,1)S(1)} %get-tuple-element.231, (s32[]{:T(128)}, s32[]{:T(128)}, bf16[4,2048,4,256]{3,1,2,0:T(8,128)(2,1)}, s32[]{:T(128)}, bf16[16,32,2048]{2,1,0:T(8,128)(2,1)}, ...), branch_computations={%region_1.1_spmd, %region_2.6_spmd} | conditional | flops 554958848 | bytes 21918928 | solution.py:82
  388.0 1.7 dynamic-slice_bitcast_fusion
  391.4 1.1 fusion.2
  394.9 8.3 %conditional.2 = (bf16[16,32,2048]{2,1,0:T(8,128)(2,1)S(1)}) conditional(s32[]{:T(128)} %convert_element_type.37, bf16[16,32,2048]{2,1,0:T(8,128)(2,1)S(1)} %get-tuple-element.231, (s32[]{:T(128)}, s32[]{:T(128)}, bf16[4,2048,4,256]{3,1,2,0:T(8,128)(2,1)}, s32[]{:T(128)}, bf16[16,32,2048]{2,1,0:T(8,128)(2,1)}, ...), branch_computations={%region_1.1_spmd, %region_2.6_spmd} | conditional | flops 554958848 | bytes 21918928 | solution.py:82
  398.2 1.7 dynamic-slice_bitcast_fusion
  401.6 1.1 fusion.2
  405.1 8.3 %conditional.2 = (bf16[16,32,2048]{2,1,0:T(8,128)(2,1)S(1)}) conditional(s32[]{:T(128)} %convert_element_type.37, bf16[16,32,2048]{2,1,0:T(8,128)(2,1)S(1)} %get-tuple-element.231, (s32[]{:T(128)}, s32[]{:T(128)}, bf16[4,2048,4,256]{3,1,2,0:T(8,128)(2,1)}, s32[]{:T(128)}, bf16[16,32,2048]{2,1,0:T(8,128)(2,1)}, ...), branch_computations={%region_1.1_spmd, %region_2.6_spmd} | conditional | flops 554958848 | bytes 21918928 | solution.py:82
  408.4 1.7 dynamic-slice_bitcast_fusion
  411.8 1.1 fusion.2
  415.3 8.3 %conditional.2 = (bf16[16,32,2048]{2,1,0:T(8,128)(2,1)S(1)}) conditional(s32[]{:T(128)} %convert_element_type.37, bf16[16,32,2048]{2,1,0:T(8,128)(2,1)S(1)} %get-tuple-element.231, (s32[]{:T(128)}, s32[]{:T(128)}, bf16[4,2048,4,256]{3,1,2,0:T(8,128)(2,1)}, s32[]{:T(128)}, bf16[16,32,2048]{2,1,0:T(8,128)(2,1)}, ...), branch_computations={%region_1.1_spmd, %region_2.6_spmd} | conditional | flops 554958848 | bytes 21918928 | solution.py:82
  418.6 1.7 dynamic-slice_bitcast_fusion
  425.5 8.3 %conditional.2 = (bf16[16,32,2048]{2,1,0:T(8,128)(2,1)S(1)}) conditional(s32[]{:T(128)} %convert_element_type.37, bf16[16,32,2048]{2,1,0:T(8,128)(2,1)S(1)} %get-tuple-element.231, (s32[]{:T(128)}, s32[]{:T(128)}, bf16[4,2048,4,256]{3,1,2,0:T(8,128)(2,1)}, s32[]{:T(128)}, bf16[16,32,2048]{2,1,0:T(8,128)(2,1)}, ...), branch_computations={%region_1.1_spmd, %region_2.6_spmd} | conditional | flops 554958848 | bytes 21918928 | solution.py:82
  428.8 1.7 dynamic-slice_bitcast_fusion
  432.2 1.1 fusion.2
  435.7 8.3 %conditional.2 = (bf16[16,32,2048]{2,1,0:T(8,128)(2,1)S(1)}) conditional(s32[]{:T(128)} %convert_element_type.37, bf16[16,32,2048]{2,1,0:T(8,128)(2,1)S(1)} %get-tuple-element.231, (s32[]{:T(128)}, s32[]{:T(128)}, bf16[4,2048,4,256]{3,1,2,0:T(8,128)(2,1)}, s32[]{:T(128)}, bf16[16,32,2048]{2,1,0:T(8,128)(2,1)}, ...), branch_computations={%region_1.1_spmd, %region_2.6_spmd} | conditional | flops 554958848 | bytes 21918928 | solution.py:82
  439.0 1.7 dynamic-slice_bitcast_fusion
  442.4 1.1 fusion.2
  445.9 8.3 %conditional.2 = (bf16[16,32,2048]{2,1,0:T(8,128)(2,1)S(1)}) conditional(s32[]{:T(128)} %convert_element_type.37, bf16[16,32,2048]{2,1,0:T(8,128)(2,1)S(1)} %get-tuple-element.231, (s32[]{:T(128)}, s32[]{:T(128)}, bf16[4,2048,4,256]{3,1,2,0:T(8,128)(2,1)}, s32[]{:T(128)}, bf16[16,32,2048]{2,1,0:T(8,128)(2,1)}, ...), branch_computations={%region_1.1_spmd, %region_2.6_spmd} | conditional | flops 554958848 | bytes 21918928 | solution.py:82
  449.2 1.7 dynamic-slice_bitcast_fusion
  456.1 8.3 %conditional.2 = (bf16[16,32,2048]{2,1,0:T(8,128)(2,1)S(1)}) conditional(s32[]{:T(128)} %convert_element_type.37, bf16[16,32,2048]{2,1,0:T(8,128)(2,1)S(1)} %get-tuple-element.231, (s32[]{:T(128)}, s32[]{:T(128)}, bf16[4,2048,4,256]{3,1,2,0:T(8,128)(2,1)}, s32[]{:T(128)}, bf16[16,32,2048]{2,1,0:T(8,128)(2,1)}, ...), branch_computations={%region_1.1_spmd, %region_2.6_spmd} | conditional | flops 554958848 | bytes 21918928 | solution.py:82
  459.4 1.7 dynamic-slice_bitcast_fusion
  464.4 1.5 broadcast_select_fusion
  (320 shorter events, 91.4 us)
Async XLA Ops:
  6.5 4.8 %copy-start = (bf16[16,32,4,256]{3,2,1,0:T(4,128)(2,1)S(1)}, bf16[16,32,4,256]{3,2,1,0:T(4,128)(2,1)}, u32[]{:S(2)}) copy-start(bf16[16,32,4,256]{3,2,1,0:T(4,128)(2,1)} %param.10) | copy-start | bytes 3145732
  6.5 294.4 %all-gather.2.cloned.1.call-start = ((), (), s32[]{:S(2)}) async-start(), calls=%async_computation | async-start | bytes 20971520 | tf_op jit(solution)/shard_map/all_gather | solution.py:66
  11.3 1.6 copy-start.3
  11.3 289.9 %copy-start.4 = (s32[16]{0:T(128)S(1)}, s32[16]{0:T(128)}, u32[]{:S(2)}) copy-start(s32[16]{0:T(128)} %param.13) | copy-start | bytes 196
  304.8 0.6 copy-start.1
  309.8 1.2 copy-start.2
  315.0 0.6 copy-start.1
  320.0 1.2 copy-start.2
  325.2 0.6 copy-start.1
  330.2 1.2 copy-start.2
  335.4 0.6 copy-start.1
  340.4 1.2 copy-start.2
  345.6 0.6 copy-start.1
  350.6 1.2 copy-start.2
  355.8 0.6 copy-start.1
  360.8 1.2 copy-start.2
  366.0 0.6 copy-start.1
  371.0 1.2 copy-start.2
  376.2 0.6 copy-start.1
  381.2 1.2 copy-start.2
  386.4 0.6 copy-start.1
  391.4 1.2 copy-start.2
  396.6 0.6 copy-start.1
  401.6 1.2 copy-start.2
  406.8 0.6 copy-start.1
  411.8 1.2 copy-start.2
  417.0 0.6 copy-start.1
  422.0 1.2 copy-start.2
  427.2 0.6 copy-start.1
  432.2 1.2 copy-start.2
  437.4 0.6 copy-start.1
  442.4 1.2 copy-start.2
  447.6 0.6 copy-start.1
  452.6 1.2 copy-start.2
  457.8 0.6 copy-start.1
  462.8 1.2 copy-start.2
Sparse Core Ops, SparseCore 0:
  11.4 289.4 all-gather.1
where the time goes:
time: 475 us; the launch traced here: 473 us
  waiting for transfers between devices  288 us (61%)
  local copies, waits for them, and re-layouts  82.7 us (17%)
  matrix products  40 us (8%)
  loops' own time  32.2 us (7%)
  other arithmetic  16.4 us (3%)
  between operations  13.5 us (3%)
    all_gather x1, waiting for transfers between devices, shards(): piece = lax.all_gather(prompt_kv, 'seq', axis=0, tiled=True)  288 us
    dynamic_slice x16, local copies, waits for them, and re-layouts, compute(): lax.dynamic_slice_in_dim(whole_prompt, first_head, kv_needed, 1)  27.7 us
    cond x96, local copies, waits for them, and re-layouts  24.5 us
    another operation x1, loops' own time, shards(): lax.fori_loop(0, holders, one_response, jnp.zeros(queries.shape, jnp.bflo...  20.4 us
    dot_general x16, matrix products, attend(): jnp.einsum('kgts,skd->tkgd', prompt_weights, prompt_pairs[:, :, head_size...  18.2 us
    reduce_sum x32, other arithmetic, attend(): denominator = jnp.sum(prompt_exp, axis=-1) + jnp.sum(own_exp, axis=-1)  14.4 us
    dot_general x16, matrix products, attend(): jnp.einsum('tkgd,skd->kgts', query, prompt_pairs[:, :, :head_size], prefe...  12.5 us
    squeeze x16, local copies, waits for them, and re-layouts, compute(): pairs_rows = lax.dynamic_index_in_dim(own_pairs, index, 0, keepdims=False)  12.3 us
  transfers between devices with their start and end apart: 1, of which 1 were waited for; matrix products, arithmetic and copies ran while one was open for 0% of the time, Pallas kernels for 0%

commit v1 on v0

v1 whole, which is shorter than its diff:
```python
import functools
import math

import jax
import jax.numpy as jnp
from jax import lax
from jax.experimental import pallas as pl
from jax.experimental.pallas import tpu as pltpu
from jax.sharding import PartitionSpec as P

QHEADS = 64
KVH = 8
HD = 128
LOG2E = math.log2(math.e)


def one_head(q_tile, own_tile, kv_buf, vt_buf, length, per_kv, plen, s_buf):
    rlen = q_tile.shape[0]
    cols = per_kv * rlen
    block = 256
    scale = HD ** -0.5 * LOG2E
    q_rows = jnp.concatenate([q_tile[:, g * HD:(g + 1) * HD] for g in range(per_kv)], axis=0)
    nt = (((1,), (1,)), ((), ()))
    own = lax.dot_general(own_tile[:, :HD], q_rows, nt, preferred_element_type=jnp.float32)
    own_at = lax.broadcasted_iota(jnp.int32, (rlen, cols), 0)
    token_at = lax.broadcasted_iota(jnp.int32, (rlen, cols), 1) % rlen
    own = jnp.where(own_at <= token_at, own, -1e30)
    peak = jnp.max(own, axis=0, keepdims=True)
    for at in range(0, plen, block):
        part = lax.dot_general(kv_buf[at:at + block, :HD], q_rows, nt, preferred_element_type=jnp.float32)
        s_buf[at:at + block, :] = part
        peak = jnp.maximum(peak, jnp.max(part, axis=0, keepdims=True))
    own_exp = jnp.exp2((own - peak) * scale)
    total = jnp.sum(own_exp, axis=0, keepdims=True)
    tn = (((0,), (0,)), ((), ()))
    acc = lax.dot_general(own_tile[:, HD:], own_exp.astype(jnp.bfloat16), tn, preferred_element_type=jnp.float32)
    for at in range(0, plen, block):
        part = jnp.exp2((s_buf[at:at + block, :] - peak) * scale)
        total = total + jnp.sum(part, axis=0, keepdims=True)
        acc = acc + jnp.dot(vt_buf[:, at:at + block], part.astype(jnp.bfloat16), preferred_element_type=jnp.float32)
    out = (acc / total).T
    alive = lax.broadcasted_iota(jnp.int32, (rlen, HD), 0) < length
    return [jnp.where(alive, out[g * rlen:(g + 1) * rlen, :], 0.0).astype(jnp.bfloat16) for g in range(per_kv)]


def attend_kernel(load_kv, n_cand, per_kv, head, cap, meta, q_ref, own_ref, *rest):
    cands = rest[:n_cand]
    out_ref = rest[n_cand + 1]
    q_buf, own_buf, kv_buf, vt_buf, s_buf, o_buf, q_sem, own_sem, kv_sem, o_sem = rest[n_cand + 2:]
    plen = kv_buf.shape[0]
    width = per_kv * HD
    lanes = pl.ds(head * width, width)
    count = meta[0]

    def q_copy(i, slot):
        return pltpu.make_async_copy(q_ref.at[meta[1 + i], :, lanes], q_buf.at[slot], q_sem.at[slot])

    def own_copy(i, slot):
        return pltpu.make_async_copy(own_ref.at[meta[1 + i]], own_buf.at[slot], own_sem.at[slot])

    def o_copy(i, slot):
        return pltpu.make_async_copy(o_buf.at[slot], out_ref.at[meta[1 + i], :, lanes], o_sem.at[slot])

    @pl.when(count > 0)
    def _():
        q_copy(0, 0).start()
        own_copy(0, 0).start()

        def step(i, before):
            slot = lax.rem(i, 2)
            source = meta[1 + cap + i]

            @pl.when(i + 1 < count)
            def _():
                q_copy(i + 1, 1 - slot).start()
                own_copy(i + 1, 1 - slot).start()

            @pl.when(source != before)
            def _():
                load_kv(cands, source, kv_buf, kv_sem)
                vt_buf[...] = kv_buf[:, HD:].T

            q_copy(i, slot).wait()
            own_copy(i, slot).wait()

            @pl.when(i >= 2)
            def _():
                o_copy(i, slot).wait()

            parts = one_head(q_buf[slot], own_buf[slot], kv_buf, vt_buf, meta[1 + 2 * cap + i], per_kv, plen, s_buf)
            for g in range(per_kv):
                o_buf[slot, :, g * HD:(g + 1) * HD] = parts[g]
            o_copy(i, slot).start()
            return source

        lax.fori_loop(0, count, step, jnp.int32(-1))
        o_copy(0, 0).wait()

        @pl.when(count > 1)
        def _():
            o_copy(0, 1).wait()


def load_stacked(cands, source, kv_buf, kv_sem):
    copy = pltpu.make_async_copy(cands[0].at[source], kv_buf, kv_sem)
    copy.start()
    copy.wait()


def attend(meta, cap, queries, own, cands, out, head, per_kv, plen, load_kv):
    rlen = queries.shape[1]
    width = per_kv * HD
    cols = per_kv * rlen
    hbm = pl.BlockSpec(memory_space=pl.ANY)
    n_cand = len(cands)
    return pl.pallas_call(
        functools.partial(attend_kernel, load_kv, n_cand, per_kv, head, cap),
        out_shape=jax.ShapeDtypeStruct(out.shape, out.dtype),
        in_specs=[pl.BlockSpec(memory_space=pltpu.SMEM)] + [hbm] * (3 + n_cand),
        out_specs=hbm,
        input_output_aliases={3 + n_cand: 0},
        scratch_shapes=[
            pltpu.VMEM((2, rlen, width), jnp.bfloat16),
            pltpu.VMEM((2, rlen, 2 * HD), jnp.bfloat16),
            pltpu.VMEM((plen, 2 * HD), jnp.bfloat16),
            pltpu.VMEM((HD, plen), jnp.bfloat16),
            pltpu.VMEM((plen, cols), jnp.float32),
            pltpu.VMEM((2, rlen, width), jnp.bfloat16),
            pltpu.SemaphoreType.DMA((2,)),
            pltpu.SemaphoreType.DMA((2,)),
            pltpu.SemaphoreType.DMA,
            pltpu.SemaphoreType.DMA((2,)),
        ],
        compiler_params=pltpu.CompilerParams(vmem_limit_bytes=32 * 1024 * 1024),
        cost_estimate=pl.CostEstimate(flops=1 << 31, bytes_accessed=1 << 23, transcendentals=1 << 23),
    )(meta, queries, own, *cands, out)


def ranked(valid, key, source, lengths):
    n = valid.shape[0]
    at = jnp.arange(n)
    key = jnp.where(valid, key, 1 << 20) * n + at
    rank = jnp.sum((key[None, :] < key[:, None]).astype(jnp.int32), axis=1)
    place = rank[None, :] == at[:, None]

    def put(values):
        return jnp.sum(jnp.where(place, values[None, :], 0), axis=1)

    return jnp.concatenate([jnp.sum(valid.astype(jnp.int32))[None], put(at), put(source), put(lengths)]).astype(jnp.int32)


def shards(queries, resp_kv, prompt_kv, lengths, group_of):
    local_heads = queries.shape[2] // HD
    group = QHEADS // KVH
    kv_needed = max(local_heads // group, 1)
    per_kv = local_heads // kv_needed
    first_head = lax.axis_index("pp") * local_heads // group
    plen = prompt_kv.shape[1]
    cap = group_of.shape[0]
    meta = ranked(jnp.ones((cap,), bool), group_of, group_of, lengths)
    out = jnp.zeros(queries.shape, jnp.bfloat16)
    for head in range(kv_needed):
        mine = lax.dynamic_index_in_dim(prompt_kv, first_head + head, 2, keepdims=False)
        own = lax.dynamic_index_in_dim(resp_kv, first_head + head, 2, keepdims=False)
        whole = lax.all_gather(mine, "seq", axis=0, tiled=True)
        out = attend(meta, cap, queries, own, [whole], out, head, per_kv, plen, load_stacked)
    return out


def solution(mesh):
    placed = (
        P(("rep", "seq"), None, ("tp", "pp")),
        P(("rep", "seq"), None, "tp", None),
        P(("rep", "seq"), None, "tp", None),
        P(("rep", "seq")),
        P(("rep", "seq")),
    )
    return jax.shard_map(
        shards,
        mesh=mesh,
        in_specs=placed,
        out_specs=P(("rep", "seq"), None, ("tp", "pp")),
        check_vma=False,
    )
```

time: 475 us -> 212 us (0.45)
  waiting for transfers between devices: 288 us -> 134 us
  local copies, waits for them, and re-layouts: 82.7 us -> 17.2 us
  Pallas kernels: 0 us -> 46.4 us
  matrix products: 40 us -> 0 us
  loops' own time: 32.2 us -> 0 us
  other arithmetic: 16.4 us -> 0.42 us
    all_gather x1 -> x2, waiting for transfers between devices: 288 us -> 134 us  [shards(): whole = lax.all_gather(mine, 'seq', axis=0, tiled=True)]
    pallas_call x0 -> x2, Pallas kernels: none -> 46.4 us  [attend(): pl.pallas_call(functools.partial(attend_kernel, load_kv, n_cand, per_kv,...]
    dot_general x64 -> x0, matrix products: 40 us -> none  [the longest x16 18.2 us: attend(): jnp.einsum('kgts,skd->tkgd', prompt_weights, prompt_pairs[:, :, head_size...]
    another operation x17 -> x0, loops' own time: 32.2 us -> none  [the longest x1 20.4 us: shards(): lax.fori_loop(0, holders, one_response, jnp.zeros(queries.shape, jnp.bflo...]
    dynamic_slice x33 -> x2, local copies, waits for them, and re-layouts: 37.9 us -> 8.67 us  [the longest x1 7.44 us: shards(): lax.dynamic_index_in_dim(prompt_kv, first_head + head, 2, keepdims=False)]
    cond x96 -> x0, local copies, waits for them, and re-layouts: 24.5 us -> none
    reduce_sum x32 -> x2, other arithmetic: 14.4 us -> 0.33 us  [the longest x1 0.18 us: ranked(): rank = jnp.sum((key[None, :] < key[:, None]).astype(jnp.int32), axis=1)]
    squeeze x16 -> x1, local copies, waits for them, and re-layouts: 12.3 us -> 0.13 us  [shards(): lax.dynamic_index_in_dim(resp_kv, first_head + head, 2, keepdims=False)]
  transfers between devices with their start and end apart: 1 -> 2, of which waited for: 1 -> 2; matrix products, arithmetic and copies ran while one was open for 0% -> 2% of each run, Pallas kernels for 0% -> 11%
where the time goes in v1:
time: 212 us
  waiting for transfers between devices  134 us (63%)
  Pallas kernels  46.4 us (22%)
  local copies, waits for them, and re-layouts  17.2 us (8%)
  between operations  13.5 us (6%)
    all_gather x2, waiting for transfers between devices, shards(): whole = lax.all_gather(mine, 'seq', axis=0, tiled=True)  134 us
    pallas_call x2, Pallas kernels, attend(): pl.pallas_call(functools.partial(attend_kernel, load_kv, n_cand, per_kv,...  46.4 us
    dynamic_slice x1, local copies, waits for them, and re-layouts, shards(): lax.dynamic_index_in_dim(prompt_kv, first_head + head, 2, keepdims=False)  7.44 us
    unnamed x14, local copies, waits for them, and re-layouts  6.81 us
  transfers between devices with their start and end apart: 2, of which 2 were waited for; matrix products, arithmetic and copies ran while one was open for 2% of the time, Pallas kernels for 11%

profile of v1, /device:TPU:0, one launch (start us, length us, event | category | flops | bytes accessed | tf_op | source)
XLA Modules:
  0.0 211.9 jit_solution(14693887997384047932)
XLA Ops:
  6.5 0.0 all-gather.7.cloned.1.call-start
  6.5 7.4 %constant_dynamic-slice_fusion = (bf16[1,2048,1,256]{3,2,1,0:T(2,128)(2,1)S(1)}, bf16[1,2048,1,256]{3,2,1,0:T(2,128)(2,1)S(1)}) fusion(bf16[1,2048,4,256]{3,2,1,0:T(4,128)(2,1)} %param.7, s32[]{:T(128)S(6)} %select_n.32, s32[]{:T(128)S(6)} %select_n.31), kind=kLoop, calls=%fused_computation.7 | loop fusion | bytes 4194312 | tf_op jit(solution)/shard_map/jit(dynamic_index_in_dim)/dynamic_slice | solution.py:163
  14.0 1.2 copy.25
  15.2 0.0 all-gather.7.cloned.1.call-update
  15.2 0.0 all-gather.5.cloned.1.call-start
  15.2 0.0 copy-start.4
  15.3 0.0 copy-start.5
  15.3 0.0 copy-start.3
  15.3 1.2 copy.23
  16.5 0.0 all-gather.5.cloned.1.call-update
  16.5 0.0 copy-done.4
  16.5 0.2 convert_reduce_fusion
  16.7 0.0 copy-done.5
  16.7 0.2 select_reduce_fusion.2
  16.9 0.1 pad_add_fusion.meta
  17.0 0.0 copy-done.3
  17.0 1.2 constant_dynamic-slice_fusion.1
  18.2 0.0 copy-start.2
  18.2 0.1 copy_bitcast_fusion
  18.4 80.5 %all-gather.7.cloned.1.call-done = bf16[4,2048,1,256]{3,1,2,0:T(8,128)(2,1)} async-done(((bf16[1,2048,1,256]{3,1,2,0:T(8,128)(2,1)}), bf16[4,2048,1,256]{3,1,2,0:T(8,128)(2,1)}) %all-gather.7.cloned.1.call-update) | async-done | bytes 4194320 | tf_op jit(solution)/shard_map/all_gather | solution.py:165
  98.8 1.6 broadcast_in_dim.41.rest_1_
  100.4 0.0 copy-done.2
  100.4 0.0 copy-start
  100.4 2.2 %copy-done = bf16[4,2048,1,256]{3,1,2,0:T(8,128)(2,1)S(1)} copy-done((bf16[4,2048,1,256]{3,1,2,0:T(8,128)(2,1)S(1)}, bf16[4,2048,1,256]{3,1,2,0:T(8,128)(2,1)}, u32[]{:S(2)}) %copy-start) | copy-done | bytes 4194328
  102.6 23.2 %shard_map.55.rest_1_ = bf16[16,32,2048]{2,1,0:T(8,128)(2,1)} custom-call(s32[49]{0:T(128)S(1)} %pad_add_fusion.meta, bf16[16,32,2048]{2,1,0:T(8,128)(2,1)S(1)} %copy-done.2, bf16[16,32,256]{2,1,0:T(8,128)(2,1)S(1)} %get-tuple-element.12.own_ref, bf16[4,2048,256]{2,1,0:T(8,128)(2,1)S(1)} %bitcast.6, ...), custom_call_target="tpu_custom_call", output_to_operand_aliasing={{}: (4, {})} | custom-call | flops 2147483648 | bytes 8388608 | tf_op jit(solution)/shard_map/pallas_call | solution.py:116
  125.8 53.9 %all-gather.5.cloned.1.call-done = bf16[4,2048,1,256]{3,1,2,0:T(8,128)(2,1)} async-done(((bf16[1,2048,1,256]{3,1,2,0:T(8,128)(2,1)}), bf16[4,2048,1,256]{3,1,2,0:T(8,128)(2,1)}) %all-gather.5.cloned.1.call-update) | async-done | bytes 4194320 | tf_op jit(solution)/shard_map/all_gather | solution.py:165
  179.7 0.0 copy-start.1
  179.7 2.2 %copy-done.1 = bf16[4,2048,1,256]{3,1,2,0:T(8,128)(2,1)S(1)} copy-done((bf16[4,2048,1,256]{3,1,2,0:T(8,128)(2,1)S(1)}, bf16[4,2048,1,256]{3,1,2,0:T(8,128)(2,1)}, u32[]{:S(2)}) %copy-start.1) | copy-done | bytes 4194328
  181.9 23.2 %shard_map.56 = bf16[16,32,2048]{2,1,0:T(8,128)(2,1)} custom-call(s32[49]{0:T(128)S(1)} %pad_add_fusion.meta, bf16[16,32,2048]{2,1,0:T(8,128)(2,1)S(1)} %copy-done.2, bf16[16,32,256]{2,1,0:T(8,128)(2,1)S(1)} %get-tuple-element.13.own_ref, bf16[4,2048,256]{2,1,0:T(8,128)(2,1)S(1)} %bitcast.7, ...), custom_call_target="tpu_custom_call", output_to_operand_aliasing={{}: (4, {})} | custom-call | flops 2147483648 | bytes 8388608 | tf_op jit(solution)/shard_map/pallas_call | solution.py:116
  (1 shorter events, 0.0 us)
Async XLA Ops:
  6.5 92.3 %all-gather.7.cloned.1.call-start = ((), (), s32[]{:S(2)}) async-start(), calls=%async_computation.1 | async-start | bytes 5242880 | tf_op jit(solution)/shard_map/all_gather | solution.py:165
  15.2 164.5 %all-gather.5.cloned.1.call-start = ((), (), s32[]{:S(2)}) async-start(), calls=%async_computation | async-start | bytes 5242880 | tf_op jit(solution)/shard_map/all_gather | solution.py:165
  15.2 1.3 copy-start.4
  15.3 1.5 copy-start.5
  15.3 1.7 copy-start.3
  18.2 82.2 %copy-start.2 = (bf16[16,32,2048]{2,1,0:T(8,128)(2,1)S(1)}, bf16[16,32,2048]{2,1,0:T(8,128)(2,1)}, u32[]{:S(2)}) copy-start(bf16[16,32,2048]{2,1,0:T(8,128)(2,1)} %q_ref.3) | copy-start | bytes 6291460
  100.4 2.2 %copy-start = (bf16[4,2048,1,256]{3,1,2,0:T(8,128)(2,1)S(1)}, bf16[4,2048,1,256]{3,1,2,0:T(8,128)(2,1)}, u32[]{:S(2)}) copy-start(bf16[4,2048,1,256]{3,1,2,0:T(8,128)(2,1)} %all-gather.7.cloned.1.call-done) | copy-start | bytes 12582916
  179.7 2.2 %copy-start.1 = (bf16[4,2048,1,256]{3,1,2,0:T(8,128)(2,1)S(1)}, bf16[4,2048,1,256]{3,1,2,0:T(8,128)(2,1)}, u32[]{:S(2)}) copy-start(bf16[4,2048,1,256]{3,1,2,0:T(8,128)(2,1)} %all-gather.5.cloned.1.call-done) | copy-start | bytes 12582916
Sparse Core Ops, SparseCore 0:
  15.3 83.4 all-gather.6
  100.4 79.2 all-gather.4

commit v2 on v1

v2 whole, which is shorter than its diff:
```python
import functools
import math

import jax
import jax.numpy as jnp
from jax import lax
from jax.experimental import pallas as pl
from jax.experimental.pallas import tpu as pltpu
from jax.sharding import PartitionSpec as P

QHEADS = 64
KVH = 8
HD = 128
LOG2E = math.log2(math.e)
VMEM_BYTES = 56 * 1024 * 1024
SLOTS = 8
HBM = pl.BlockSpec(memory_space=pl.ANY)
SMEM = pl.BlockSpec(memory_space=pltpu.SMEM)


def one_head(q_tile, own_tile, kv_buf, vt_buf, length, per_kv, plen, s_buf):
    rlen = q_tile.shape[0]
    cols = per_kv * rlen
    block = 256
    scale = HD ** -0.5 * LOG2E
    q_rows = jnp.concatenate([q_tile[:, g * HD:(g + 1) * HD] for g in range(per_kv)], axis=0)
    nt = (((1,), (1,)), ((), ()))
    own = lax.dot_general(own_tile[:, :HD], q_rows, nt, preferred_element_type=jnp.float32)
    own_at = lax.broadcasted_iota(jnp.int32, (rlen, cols), 0)
    token_at = lax.broadcasted_iota(jnp.int32, (rlen, cols), 1) % rlen
    own = jnp.where(own_at <= token_at, own, -1e30)
    peak = jnp.max(own, axis=0, keepdims=True)
    for at in range(0, plen, block):
        part = lax.dot_general(kv_buf[at:at + block, :HD], q_rows, nt, preferred_element_type=jnp.float32)
        s_buf[at:at + block, :] = part
        peak = jnp.maximum(peak, jnp.max(part, axis=0, keepdims=True))
    own_exp = jnp.exp2((own - peak) * scale)
    total = jnp.sum(own_exp, axis=0, keepdims=True)
    tn = (((0,), (0,)), ((), ()))
    acc = lax.dot_general(own_tile[:, HD:], own_exp.astype(jnp.bfloat16), tn, preferred_element_type=jnp.float32)
    for at in range(0, plen, block):
        part = jnp.exp2((s_buf[at:at + block, :] - peak) * scale)
        total = total + jnp.sum(part, axis=0, keepdims=True)
        acc = acc + jnp.dot(vt_buf[:, at:at + block], part.astype(jnp.bfloat16), preferred_element_type=jnp.float32)
    out = (acc / total).T
    alive = lax.broadcasted_iota(jnp.int32, (rlen, HD), 0) < length
    return [jnp.where(alive, out[g * rlen:(g + 1) * rlen, :], 0.0).astype(jnp.bfloat16) for g in range(per_kv)]


def listed(items, cap, count, groups, lengths, target, source, first, slots):
    def look(at, state):
        n, slot = state
        hit = groups[at] == target

        @pl.when(hit)
        def _():
            items[n] = first + (slot if slots else at)
            items[cap + n] = source
            items[2 * cap + n] = lengths[at]

        step = hit.astype(jnp.int32)
        return n + step, slot + step

    return lax.fori_loop(0, groups.shape[0], look, (count, jnp.int32(0)))[0]


def attend_kernel(passes, n_cand, per_kv, head, two, fresh, *refs):
    refs = list(refs)
    facts, groups, lengths = refs[:3]
    refs = refs[3:]
    if two:
        far_groups, far_lengths, x_ref = refs[:3]
        refs = refs[3:]
    q_ref, own_ref = refs[:2]
    cands, refs = refs[2:2 + n_cand], refs[2 + n_cand:]
    n_out = 2 if two else 1
    if not fresh:
        refs = refs[n_out:]
    outs, refs = refs[:n_out], refs[n_out:]
    items, q_buf, own_buf, kv_buf, vt_buf, s_buf, o_buf, q_sem, own_sem, kv_sem, o_sem = refs
    local = groups.shape[0]
    cap = items.shape[0] // 3
    width = per_kv * HD
    stacked = passes is None

    count = jnp.int32(0)
    if stacked:
        def one_prompt(prompt, n):
            return listed(items, cap, n, groups, lengths, prompt, prompt, 0, False)

        count = lax.fori_loop(0, cands[0].shape[0], one_prompt, count)
    else:
        for far, target, source in passes:
            if far:
                count = listed(items, cap, count, far_groups, far_lengths, facts[target], facts[source], local, True)
            else:
                count = listed(items, cap, count, groups, lengths, facts[target], facts[source], 0, False)

    def each_array(i, act_local, act_far):
        at = items[i]
        if not two:
            act_local(at)
            return

        @pl.when(at < local)
        def _():
            act_local(at)

        @pl.when(at >= local)
        def _():
            act_far(at - local)

    mine = pl.ds(head * width, width)
    first, last = pl.ds(0, width), pl.ds(width, 2 * HD)

    def fetch(i, slot):
        def here(at):
            pltpu.make_async_copy(q_ref.at[at, :, mine], q_buf.at[slot], q_sem.at[slot]).start()
            pltpu.make_async_copy(own_ref.at[at], own_buf.at[slot], own_sem.at[slot]).start()

        def far(at):
            pltpu.make_async_copy(x_ref.at[at, :, first], q_buf.at[slot], q_sem.at[slot]).start()
            pltpu.make_async_copy(x_ref.at[at, :, last], own_buf.at[slot], own_sem.at[slot]).start()

        each_array(i, here, far)

    def fetched(slot):
        pltpu.make_async_copy(q_ref.at[0, :, first], q_buf.at[slot], q_sem.at[slot]).wait()
        pltpu.make_async_copy(own_ref.at[0], own_buf.at[slot], own_sem.at[slot]).wait()

    def store(i, slot):
        def here(at):
            pltpu.make_async_copy(o_buf.at[slot], outs[0].at[at, :, mine], o_sem.at[slot]).start()

        def far(at):
            pltpu.make_async_copy(o_buf.at[slot], outs[1].at[at], o_sem.at[slot]).start()

        each_array(i, here, far)

    def stored(slot):
        pltpu.make_async_copy(o_buf.at[slot], outs[0].at[0, :, first], o_sem.at[slot]).wait()

    def load(source):
        if stacked:
            pltpu.make_async_copy(cands[0].at[source], kv_buf, kv_sem).start()
        else:
            for which in range(n_cand):
                @pl.when(source == which)
                def _():
                    pltpu.make_async_copy(cands[which], kv_buf, kv_sem).start()

        pltpu.make_async_copy(kv_buf, kv_buf, kv_sem).wait()

    @pl.when(count > 0)
    def _():
        fetch(0, 0)

        def step(i, before):
            slot = lax.rem(i, 2)
            source = items[cap + i]

            @pl.when(i + 1 < count)
            def _():
                fetch(i + 1, 1 - slot)

            @pl.when(source != before)
            def _():
                load(source)
                vt_buf[...] = kv_buf[:, HD:].T

            fetched(slot)

            @pl.when(i >= 2)
            def _():
                stored(slot)

            tiles = one_head(q_buf[slot], own_buf[slot], kv_buf, vt_buf, items[2 * cap + i], per_kv, kv_buf.shape[0], s_buf)
            for g in range(per_kv):
                o_buf[slot, :, g * HD:(g + 1) * HD] = tiles[g]
            store(i, slot)
            return source

        lax.fori_loop(0, count, step, jnp.int32(-1))
        stored(0)

        @pl.when(count > 1)
        def _():
            stored(1)


def attend(facts, groups, lengths, queries, own, cands, outs, head, per_kv, passes, items, far=None, fresh=False):
    rlen = queries.shape[1]
    plen = cands[0].shape[-2]
    width = per_kv * HD
    small = [facts, groups, lengths] + (list(far[:2]) if far else [])
    large = ([far[2]] if far else []) + [queries, own] + cands
    operands = small + large
    aliases = {}
    if not fresh:
        aliases = {len(operands) + i: i for i in range(len(outs))}
        operands += outs
    cap = groups.shape[0] + (SLOTS if far else 0)
    return pl.pallas_call(
        functools.partial(attend_kernel, passes, len(cands), per_kv, head, far is not None, fresh),
        out_shape=[jax.ShapeDtypeStruct(o.shape, o.dtype) for o in outs],
        in_specs=[SMEM] * len(small) + [HBM] * (len(operands) - len(small)),
        out_specs=[HBM] * len(outs),
        input_output_aliases=aliases,
        scratch_shapes=[
            pltpu.SMEM((3 * cap,), jnp.int32),
            pltpu.VMEM((2, rlen, width), jnp.bfloat16),
            pltpu.VMEM((2, rlen, 2 * HD), jnp.bfloat16),
            pltpu.VMEM((plen, 2 * HD), jnp.bfloat16),
            pltpu.VMEM((HD, plen), jnp.bfloat16),
            pltpu.VMEM((plen, per_kv * rlen), jnp.float32),
            pltpu.VMEM((2, rlen, width), jnp.bfloat16),
            pltpu.SemaphoreType.DMA((2,)),
            pltpu.SemaphoreType.DMA((2,)),
            pltpu.SemaphoreType.DMA,
            pltpu.SemaphoreType.DMA((2,)),
        ],
        compiler_params=pltpu.CompilerParams(vmem_limit_bytes=VMEM_BYTES),
        cost_estimate=pl.CostEstimate(flops=int(items * 1.2e9), bytes_accessed=1 << 21, transcendentals=0),
    )(*operands)


def pack_kernel(target, width, facts, groups, q_ref, own0, own1, out0, out1, sem):
    owns, outs = (own0, own1), (out0, out1)

    def copies(at, slot):
        made = []
        for head in range(2):
            made.append(pltpu.make_async_copy(
                q_ref.at[at, :, pl.ds(head * width, width)], outs[head].at[slot, :, pl.ds(0, width)], sem))
            made.append(pltpu.make_async_copy(owns[head].at[at], outs[head].at[slot, :, pl.ds(width, 2 * HD)], sem))
        return made

    def each(act):
        def look(at, slot):
            hit = groups[at] == facts[target]

            @pl.when(hit)
            def _():
                for copy in copies(at, slot):
                    act(copy)

            return slot + hit.astype(jnp.int32)

        lax.fori_loop(0, groups.shape[0], look, jnp.int32(0))

    each(lambda copy: copy.start())
    each(lambda copy: copy.wait())


def pack(facts, target, groups, queries, own, width):
    shape = jax.ShapeDtypeStruct((SLOTS, queries.shape[1], width + 2 * HD), queries.dtype)
    return pl.pallas_call(
        functools.partial(pack_kernel, target, width),
        out_shape=[shape, shape],
        in_specs=[SMEM, SMEM, HBM, HBM, HBM],
        out_specs=[HBM, HBM],
        scratch_shapes=[pltpu.SemaphoreType.DMA],
        compiler_params=pltpu.CompilerParams(vmem_limit_bytes=VMEM_BYTES),
    )(facts, groups, queries, *own)


def merge_kernel(target, width, facts, groups, got0, got1, old, out, sem):
    got = (got0, got1)

    def each(act):
        def look(at, slot):
            hit = groups[at] == facts[target]

            @pl.when(hit)
            def _():
                for head in range(2):
                    act(pltpu.make_async_copy(got[head].at[slot], out.at[at, :, pl.ds(head * width, width)], sem))

            return slot + hit.astype(jnp.int32)

        lax.fori_loop(0, groups.shape[0], look, jnp.int32(0))

    each(lambda copy: copy.start())
    each(lambda copy: copy.wait())


def merge(facts, target, groups, got, out, width):
    return pl.pallas_call(
        functools.partial(merge_kernel, target, width),
        out_shape=jax.ShapeDtypeStruct(out.shape, out.dtype),
        in_specs=[SMEM, SMEM, HBM, HBM, HBM],
        out_specs=HBM,
        input_output_aliases={4: 0},
        scratch_shapes=[pltpu.SemaphoreType.DMA],
        compiler_params=pltpu.CompilerParams(vmem_limit_bytes=VMEM_BYTES),
    )(facts, groups, *got, out)


def after(value, *others):
    return lax.optimization_barrier((value,) + others)[0]


def gathered(queries, resp_kv, prompt_kv, lengths, group_of, first_head, kv_needed, per_kv):
    out = jax.ShapeDtypeStruct(queries.shape, jnp.bfloat16)
    facts = jnp.zeros((8,), jnp.int32)
    for head in range(kv_needed):
        mine = lax.dynamic_index_in_dim(prompt_kv, first_head + head, 2, keepdims=False)
        own = lax.dynamic_index_in_dim(resp_kv, first_head + head, 2, keepdims=False)
        whole = lax.all_gather(mine, "seq", axis=0, tiled=True)
        [out] = attend(facts, group_of, lengths, queries, own, [whole], [out], head, per_kv, None, 16, fresh=head == 0)
    return out


def relayed(queries, resp_kv, prompt_kv, lengths, group_of, first_head, per_kv):
    me = lax.axis_index("seq")
    width = per_kv * HD
    middle, inward, outward = [(1, 2), (2, 1)], [(0, 1), (3, 2)], [(1, 0), (2, 3)]

    def send(pairs, value):
        return lax.ppermute(value, "seq", pairs)

    by_head = after(jnp.transpose(prompt_kv[0], (1, 0, 2)))
    mine, mid, inn, out_got = [], [], [], []
    for head in range(2):
        mine.append(lax.dynamic_index_in_dim(by_head, first_head + head, 0, keepdims=False))
        inn.append(send(inward, mine[head]))
        mid.append(send(middle, mine[head]))
        out_got.append(send(outward, mine[head]))
    far_groups, far_lengths = send(inward, group_of), send(inward, lengths)

    low = me < 2
    is_inner = (me == 1) | (me == 2)
    outer, inner = jnp.where(low, 0, 3), jnp.where(low, 1, 2)
    far_inner, far_outer = jnp.where(low, 2, 1), jnp.where(low, 3, 0)
    facts = jnp.stack([
        me,
        jnp.zeros_like(me),
        jnp.where(is_inner, outer, inner),
        jnp.where(is_inner, 0, 2),
        jnp.where(is_inner, far_inner, -1),
        jnp.ones_like(me),
        jnp.where(is_inner, far_outer, -1),
        jnp.where(is_inner, far_outer, far_inner),
        jnp.where(is_inner, 0, 1),
        jnp.where(is_inner, -1, far_outer),
    ]).astype(jnp.int32)

    own_by_head = after(jnp.transpose(resp_kv, (2, 0, 1, 3)))
    own = [lax.dynamic_index_in_dim(own_by_head, first_head + head, 0, keepdims=False) for head in range(2)]
    packed = pack(facts, 9, group_of, queries, own, width)
    out = jax.ShapeDtypeStruct(queries.shape, jnp.bfloat16)
    back_shape = jax.ShapeDtypeStruct((SLOTS, queries.shape[1], width), jnp.bfloat16)

    def run(head, cands, outs, passes, items, far=None, fresh=False):
        return attend(facts, group_of, lengths, queries, own[head], cands, outs, head, per_kv, passes, items, far, fresh)

    for head in range(2):
        [out] = run(head, [mine[head]], [out], [(False, 0, 1)], 4, fresh=head == 0)
    mid.append(send(middle, inn[0]))
    mid.append(send(middle, inn[1]))
    out_got.append(send(outward, mid[0]))
    out_got.append(send(outward, mid[1]))
    far = [send(inward, after(packed[head], inn[1])) for head in range(2)]
    for head in range(2):
        [out] = run(head, [inn[head], mid[head], out_got[head]], [out], [(False, 2, 3), (False, 4, 5)], 8)
    back = [None, None]
    far_all = [(far_groups, far_lengths, far[head]) for head in range(2)]
    zeros = jnp.zeros(back_shape.shape, back_shape.dtype)
    out, back[0] = run(0, [mid[2], out_got[2]], [out, zeros], [(True, 6, 1), (False, 7, 8)], 8, far_all[0])
    back[0] = send(outward, back[0])
    out, back[1] = run(1, [mid[3]], [out, zeros], [(True, 6, 1)], 4, far_all[1])
    back[1] = send(outward, back[1])
    [out] = run(1, [mid[3], out_got[3]], [out], [(False, 7, 8)], 4)
    return merge(facts, 9, group_of, back, out, width)


def shards(queries, resp_kv, prompt_kv, lengths, group_of):
    local_heads = queries.shape[2] // HD
    group = QHEADS // KVH
    kv_needed = max(local_heads // group, 1)
    per_kv = local_heads // kv_needed
    first_head = lax.axis_index("pp") * local_heads // group
    args = (queries, resp_kv, prompt_kv, lengths, group_of, first_head)
    if lax.axis_size("seq") == 4 and kv_needed == 2 and prompt_kv.shape[0] == 1:
        return relayed(*args, per_kv)
    return gathered(*args, kv_needed, per_kv)


def solution(mesh):
    placed = (
        P(("rep", "seq"), None, ("tp", "pp")),
        P(("rep", "seq"), None, "tp", None),
        P(("rep", "seq"), None, "tp", None),
        P(("rep", "seq")),
        P(("rep", "seq")),
    )
    return jax.shard_map(
        shards,
        mesh=mesh,
        in_specs=placed,
        out_specs=P(("rep", "seq"), None, ("tp", "pp")),
        check_vma=False,
    )
```

time: 212 us -> 218 us (1.028)
  the two profiles are of different devices: /device:TPU:0 before, /device:TPU:4 now
where the time goes in v2:
time: 218 us; the launch traced here: 219 us
  Pallas kernels  105 us (48%)
  starting transfers between devices  61.3 us (28%)
  waiting for transfers between devices  38.4 us (18%)
  local copies, waits for them, and re-layouts  14.2 us (7%)
    ppermute x16, starting transfers between devices, send(): return lax.ppermute(value, 'seq', pairs)  61.3 us
    pallas_call x7, Pallas kernels, attend(): pl.pallas_call(functools.partial(attend_kernel, passes, len(cands), per_k...  38.8 us
    ppermute x16, waiting for transfers between devices, send(): return lax.ppermute(value, 'seq', pairs)  38.4 us
    pallas_call x1, Pallas kernels, pack(): pl.pallas_call(functools.partial(pack_kernel, target, width), out_shape=[...  36.5 us
    pallas_call x1, Pallas kernels, merge(): pl.pallas_call(functools.partial(merge_kernel, target, width), out_shape=...  29.6 us
    unnamed x38, local copies, waits for them, and re-layouts  9.09 us
  transfers between devices with their start and end apart: 16, of which 5 were waited for; matrix products, arithmetic and copies ran while one was open for 2% of the time, Pallas kernels for 34%

profile of v2, /device:TPU:4, one launch (start us, length us, event | category | flops | bytes accessed | tf_op | source)
XLA Modules:
  0.0 219.2 jit_solution(13877438182081916603)
XLA Ops:
  0.0 4.7 %copy.19 = bf16[1,2048,4,256]{3,1,2,0:T(8,128)(2,1)} copy(bf16[1,2048,4,256]{3,2,1,0:T(4,128)(2,1)} %param.7) | data formatting | bytes 8388608 | tf_op args[2]
  4.7 1.7 dynamic-slice_bitcast_fusion
  6.4 1.3 collective-permute-start.10
  7.7 6.5 %collective-permute-start.4 = (bf16[2048,256]{1,0:T(8,128)(2,1)S(1)}, bf16[2048,256]{1,0:T(8,128)(2,1)}, u32[]{:S(2)}, u32[]{:S(2)}) collective-permute-start(bf16[2048,256]{1,0:T(8,128)(2,1)S(1)} %get-tuple-element.21.refs_5_), channel_id=1, source_target_pairs={{0,4},{12,8},{1,5},{13,9},{2,6},{14,10},{3,7},{15,11},{16,20},{28,... | collective-permute-start | bytes 3145736 | tf_op jit(solution)/shard_map/ppermute | solution.py:320
  14.2 1.6 collective-permute-start.6
  15.9 4.3 %collective-permute-start.2 = (bf16[2048,256]{1,0:T(8,128)(2,1)S(1)}, bf16[2048,256]{1,0:T(8,128)(2,1)}, u32[]{:S(2)}, u32[]{:S(2)}) collective-permute-start(bf16[2048,256]{1,0:T(8,128)(2,1)S(1)} %get-tuple-element.22.refs_5_), channel_id=1, source_target_pairs={{0,4},{12,8},{1,5},{13,9},{2,6},{14,10},{3,7},{15,11},{16,20},{28,... | collective-permute-start | bytes 3145736 | tf_op jit(solution)/shard_map/ppermute | solution.py:320
  20.2 1.6 collective-permute-start.8
  21.8 1.4 copy.20
  23.2 0.6 stack.35.facts.refs_0_
  23.8 0.9 dynamic-slice_bitcast_fusion.2
  24.7 13.3 %shard_map.56.refs_6_ = bf16[16,32,2048]{2,1,0:T(8,128)(2,1)} custom-call(s32[10]{0:T(128)} %stack.35.facts.refs_0_, s32[16]{0:T(128)} %groups.3, s32[16]{0:T(128)} %refs_2_.13, bf16[16,32,2048]{2,1,0:T(8,128)(2,1)} %refs_3_.9, bf16[16,32,256]{2,1,0:T(8,128)(2,1)} %get-tuple-element.24.own0.refs_4_.refs_7_, bf16[2048,256]{1,0:T(8,128)(2,1)} %copy-done.1), custom_call_target="tpu_custom_call" | custom-call | flops 4800000000 | bytes 2097152 | tf_op jit(solution)/shard_map/pallas_call | solution.py:203
  38.1 1.3 collective-permute-start.9
  39.4 13.3 %shard_map.57.refs_8_ = bf16[16,32,2048]{2,1,0:T(8,128)(2,1)} custom-call(s32[10]{0:T(128)} %stack.35.facts.refs_0_, s32[16]{0:T(128)} %groups.3, s32[16]{0:T(128)} %refs_2_.13, bf16[16,32,2048]{2,1,0:T(8,128)(2,1)} %refs_3_.9, bf16[16,32,256]{2,1,0:T(8,128)(2,1)} %get-tuple-element.23.own1.refs_4_.refs_7_, ...), custom_call_target="tpu_custom_call", output_to_operand_aliasing={{}: (6, {})} | custom-call | flops 4800000000 | bytes 2097152 | tf_op jit(solution)/shard_map/pallas_call | solution.py:203
  52.7 36.5 %shard_map.55 = (bf16[8,32,1280]{2,1,0:T(8,128)(2,1)}, bf16[8,32,1280]{2,1,0:T(8,128)(2,1)}) custom-call(s32[10]{0:T(128)} %stack.35.facts.refs_0_, s32[16]{0:T(128)} %groups.3, bf16[16,32,2048]{2,1,0:T(8,128)(2,1)} %refs_3_.9, bf16[16,32,256]{2,1,0:T(8,128)(2,1)} %get-tuple-element.24.own0.refs_4_.refs_7_, ...), custom_call_target="tpu_custom_call" | custom-call | tf_op jit(solution)/shard_map/pallas_call | solution.py:257
  89.2 0.0 copy-start.5
  89.2 0.0 collective-permute-done.4.refs_5_
  89.3 0.9 collective-permute-start.5
  90.1 1.3 collective-permute-start.7
  91.4 1.1 shard_map.58.refs_8_
  92.6 0.0 collective-permute-done.2.refs_5_
  92.6 17.0 %collective-permute-start = (s32[16]{0:T(128)S(1)}, s32[16]{0:T(128)S(1)}, u32[]{:S(2)}, u32[]{:S(2)}) collective-permute-start(s32[16]{0:T(128)S(1)} %copy-done.5), channel_id=1, source_target_pairs={{0,4},{12,8},{1,5},{13,9},{2,6},{14,10},{3,7},{15,11},{16,20},{28,... | collective-permute-start | bytes 200 | tf_op jit(solution)/shard_map/ppermute | solution.py:320
  109.6 0.0 copy-start.15
  109.6 1.5 collective-permute-start.3
  111.1 0.7 collective-permute-start.13
  111.9 0.3 copy-done.10
  112.1 1.1 shard_map.59.refs_10_
  113.3 15.2 %collective-permute-start.1 = (s32[16]{0:T(128)S(1)}, s32[16]{0:T(128)S(1)}, u32[]{:S(2)}, u32[]{:S(2)}) collective-permute-start(s32[16]{0:T(128)S(1)} %copy-done.15), channel_id=1, source_target_pairs={{0,4},{12,8},{1,5},{13,9},{2,6},{14,10},{3,7},{15,11},{16,20},{28,... | collective-permute-start | bytes 200 | tf_op jit(solution)/shard_map/ppermute | solution.py:320
  128.5 1.3 collective-permute-done.1.refs_4_
  129.8 4.2 %collective-permute-start.12 = (bf16[8,32,1280]{2,1,0:T(8,128)(2,1)S(1)}, bf16[8,32,1280]{2,1,0:T(8,128)(2,1)S(1)}, u32[]{:S(2)}, u32[]{:S(2)}) collective-permute-start(bf16[8,32,1280]{2,1,0:T(8,128)(2,1)S(1)} %copy-done.11), channel_id=1, source_target_pairs={{0,4},{12,8},{1,5},{13,9},{2,6},{14,10},{3,7},{15,11},{16,20},{28,... | collective-permute-start | bytes 1966088 | tf_op jit(solution)/shard_map/ppermute | solution.py:320
  134.0 1.3 collective-permute-start.15
  135.4 1.0 broadcast_in_dim.3.clone.refs_11_
  136.4 0.2 copy-done.7
  136.5 0.3 copy-done.8
  136.8 4.5 %shard_map.60 = (bf16[16,32,2048]{2,1,0:T(8,128)(2,1)}, bf16[8,32,1024]{2,1,0:T(8,128)(2,1)}) custom-call(s32[10]{0:T(128)} %stack.35.facts.refs_0_, s32[16]{0:T(128)} %groups.3, s32[16]{0:T(128)} %refs_2_.13, s32[16]{0:T(128)} %copy-done.16, s32[16]{0:T(128)} %copy-done.17, ...), custom_call_target="tpu_custom_call", output_to_operand_aliasing={{0}: (10, {}), {1}: (11, {})} | custom-call | flops 9600000000 | bytes 2097152 | tf_op jit(solution)/shard_map/pallas_call | solution.py:203
  141.4 4.6 %collective-permute-done.12.refs_5_ = bf16[8,32,1280]{2,1,0:T(8,128)(2,1)S(1)} collective-permute-done((bf16[8,32,1280]{2,1,0:T(8,128)(2,1)S(1)}, bf16[8,32,1280]{2,1,0:T(8,128)(2,1)S(1)}, u32[]{:S(2)}, u32[]{:S(2)}) %collective-permute-start.12) | collective-permute-done | bytes 655392 | tf_op jit(solution)/shard_map/ppermute | solution.py:320
  146.0 0.9 broadcast_in_dim.3.refs_10_
  146.9 0.1 copy-done.14
  147.0 0.3 copy-done.6
  147.3 1.1 shard_map.61
  148.4 1.3 collective-permute-start.14
  149.7 1.3 collective-permute-start.11
  151.0 7.7 %collective-permute-done.15.refs_6_ = bf16[2048,256]{1,0:T(8,128)(2,1)S(1)} collective-permute-done((bf16[2048,256]{1,0:T(8,128)(2,1)}, bf16[2048,256]{1,0:T(8,128)(2,1)S(1)}, u32[]{:S(2)}, u32[]{:S(2)}) %collective-permute-start.15) | collective-permute-done | bytes 1048608 | tf_op jit(solution)/shard_map/ppermute | solution.py:320
  158.8 1.0 copy-done.9
  159.8 4.3 %shard_map.62.old = bf16[16,32,2048]{2,1,0:T(8,128)(2,1)} custom-call(s32[10]{0:T(128)} %stack.35.facts.refs_0_, s32[16]{0:T(128)} %groups.3, s32[16]{0:T(128)} %refs_2_.13, bf16[16,32,2048]{2,1,0:T(8,128)(2,1)} %refs_3_.9, bf16[16,32,256]{2,1,0:T(8,128)(2,1)} %get-tuple-element.23.own1.refs_4_.refs_7_, ...), custom_call_target="tpu_custom_call", output_to_operand_aliasing={{}: (7, {})} | custom-call | flops 4800000000 | bytes 2097152 | tf_op jit(solution)/shard_map/pallas_call | solution.py:203
  164.1 16.9 %collective-permute-done.14.got1 = bf16[8,32,1024]{2,1,0:T(8,128)(2,1)S(1)} collective-permute-done((bf16[8,32,1024]{2,1,0:T(8,128)(2,1)}, bf16[8,32,1024]{2,1,0:T(8,128)(2,1)S(1)}, u32[]{:S(2)}, u32[]{:S(2)}) %collective-permute-start.14) | collective-permute-done | bytes 524320 | tf_op jit(solution)/shard_map/ppermute | solution.py:320
  181.0 7.8 %collective-permute-done.11.got0 = bf16[8,32,1024]{2,1,0:T(8,128)(2,1)S(1)} collective-permute-done((bf16[8,32,1024]{2,1,0:T(8,128)(2,1)S(1)}, bf16[8,32,1024]{2,1,0:T(8,128)(2,1)S(1)}, u32[]{:S(2)}, u32[]{:S(2)}) %collective-permute-start.11) | collective-permute-done | bytes 524320 | tf_op jit(solution)/shard_map/ppermute | solution.py:320
  188.8 0.8 copy-done.4
  189.6 29.6 %shard_map.63 = bf16[16,32,2048]{2,1,0:T(8,128)(2,1)} custom-call(s32[10]{0:T(128)} %stack.35.facts.refs_0_, s32[16]{0:T(128)} %groups.3, bf16[8,32,1024]{2,1,0:T(8,128)(2,1)} %copy-done.4, bf16[8,32,1024]{2,1,0:T(8,128)(2,1)} %copy-done.3, bf16[16,32,2048]{2,1,0:T(8,128)(2,1)} %shard_map.62.old), custom_call_target="tpu_custom_call", output_to_operand_aliasing={{}: (4, {})} | custom-call | tf_op jit(solution)/shard_map/pallas_call | solution.py:288
  (36 shorter events, 0.1 us)
Async XLA Ops:
  6.4 18.3 %copy-start.1 = (bf16[2048,256]{1,0:T(8,128)(2,1)}, bf16[2048,256]{1,0:T(8,128)(2,1)S(1)}, u32[]{:S(2)}) copy-start(bf16[2048,256]{1,0:T(8,128)(2,1)S(1)} %get-tuple-element.21.refs_5_) | copy-start | bytes 3145732
  6.4 31.7 %copy-start = (bf16[2048,256]{1,0:T(8,128)(2,1)}, bf16[2048,256]{1,0:T(8,128)(2,1)S(1)}, u32[]{:S(2)}) copy-start(bf16[2048,256]{1,0:T(8,128)(2,1)S(1)} %get-tuple-element.22.refs_5_) | copy-start | bytes 3145732
  6.4 31.6 %collective-permute-start.10 = (bf16[2048,256]{1,0:T(8,128)(2,1)S(1)}, bf16[2048,256]{1,0:T(8,128)(2,1)}, u32[]{:S(2)}, u32[]{:S(2)}) collective-permute-start(bf16[2048,256]{1,0:T(8,128)(2,1)S(1)} %get-tuple-element.21.refs_5_), channel_id=1, source_target_pairs={{4,0},{8,12},{5,1},{9,13},{6,2},{10,14},{7,3},{11,15},{20,16},{24,... | collective-permute-start | bytes 3145736 | tf_op jit(solution)/shard_map/ppermute | solution.py:320
  7.7 81.5 %collective-permute-start.4 = (bf16[2048,256]{1,0:T(8,128)(2,1)S(1)}, bf16[2048,256]{1,0:T(8,128)(2,1)}, u32[]{:S(2)}, u32[]{:S(2)}) collective-permute-start(bf16[2048,256]{1,0:T(8,128)(2,1)S(1)} %get-tuple-element.21.refs_5_), channel_id=1, source_target_pairs={{0,4},{12,8},{1,5},{13,9},{2,6},{14,10},{3,7},{15,11},{16,20},{28,... | collective-permute-start | bytes 3145736 | tf_op jit(solution)/shard_map/ppermute | solution.py:320
  14.2 75.9 %collective-permute-start.6 = (bf16[2048,256]{1,0:T(8,128)(2,1)S(1)}, bf16[2048,256]{1,0:T(8,128)(2,1)}, u32[]{:S(2)}, u32[]{:S(2)}) collective-permute-start(bf16[2048,256]{1,0:T(8,128)(2,1)S(1)} %get-tuple-element.21.refs_5_), channel_id=1, source_target_pairs={{4,8},{8,4},{5,9},{9,5},{6,10},{10,6},{7,11},{11,7},{20,24},{24,20... | collective-permute-start | bytes 3145736 | tf_op jit(solution)/shard_map/ppermute | solution.py:320
  15.9 76.7 %collective-permute-start.2 = (bf16[2048,256]{1,0:T(8,128)(2,1)S(1)}, bf16[2048,256]{1,0:T(8,128)(2,1)}, u32[]{:S(2)}, u32[]{:S(2)}) collective-permute-start(bf16[2048,256]{1,0:T(8,128)(2,1)S(1)} %get-tuple-element.22.refs_5_), channel_id=1, source_target_pairs={{0,4},{12,8},{1,5},{13,9},{2,6},{14,10},{3,7},{15,11},{16,20},{28,... | collective-permute-start | bytes 3145736 | tf_op jit(solution)/shard_map/ppermute | solution.py:320
  20.2 89.5 %collective-permute-start.8 = (bf16[2048,256]{1,0:T(8,128)(2,1)S(1)}, bf16[2048,256]{1,0:T(8,128)(2,1)}, u32[]{:S(2)}, u32[]{:S(2)}) collective-permute-start(bf16[2048,256]{1,0:T(8,128)(2,1)S(1)} %get-tuple-element.22.refs_5_), channel_id=1, source_target_pairs={{4,8},{8,4},{5,9},{9,5},{6,10},{10,6},{7,11},{11,7},{20,24},{24,20... | collective-permute-start | bytes 3145736 | tf_op jit(solution)/shard_map/ppermute | solution.py:320
  38.1 73.0 %collective-permute-start.9 = (bf16[2048,256]{1,0:T(8,128)(2,1)S(1)}, bf16[2048,256]{1,0:T(8,128)(2,1)S(1)}, u32[]{:S(2)}, u32[]{:S(2)}) collective-permute-start(bf16[2048,256]{1,0:T(8,128)(2,1)S(1)} %get-tuple-element.22.refs_5_), channel_id=1, source_target_pairs={{4,0},{8,12},{5,1},{9,13},{6,2},{10,14},{7,3},{11,15},{20,16},{24,... | collective-permute-start | bytes 3145736 | tf_op jit(solution)/shard_map/ppermute | solution.py:320
  89.2 3.4 %copy-start.5 = (s32[16]{0:T(128)S(1)}, s32[16]{0:T(128)}, u32[]{:S(2)}) copy-start(s32[16]{0:T(128)} %groups.3) | copy-start | bytes 196
  89.2 20.4 %copy-start.12 = (bf16[8,32,1280]{2,1,0:T(8,128)(2,1)S(1)}, bf16[8,32,1280]{2,1,0:T(8,128)(2,1)}, u32[]{:S(2)}) copy-start(bf16[8,32,1280]{2,1,0:T(8,128)(2,1)} %get-tuple-element.14) | copy-start | bytes 1966084
  89.3 46.1 %collective-permute-start.5 = (bf16[2048,256]{1,0:T(8,128)(2,1)}, bf16[2048,256]{1,0:T(8,128)(2,1)S(1)}, u32[]{:S(2)}, u32[]{:S(2)}) collective-permute-start(bf16[2048,256]{1,0:T(8,128)(2,1)} %collective-permute-done.4.refs_5_), channel_id=1, source_target_pairs={{4,8},{8,4},{5,9},{9,5},{6,10},{10,6},{7,11},{11,7},{20,24},{24,20... | collective-permute-start | bytes 3145736 | tf_op jit(solution)/shard_map/ppermute | solution.py:320
  90.1 45.2 %collective-permute-start.7 = (bf16[2048,256]{1,0:T(8,128)(2,1)}, bf16[2048,256]{1,0:T(8,128)(2,1)S(1)}, u32[]{:S(2)}, u32[]{:S(2)}) collective-permute-start(bf16[2048,256]{1,0:T(8,128)(2,1)} %collective-permute-done.6.refs_6_), channel_id=1, source_target_pairs={{4,0},{8,12},{5,1},{9,13},{6,2},{10,14},{7,3},{11,15},{20,16},{24,... | collective-permute-start | bytes 3145736 | tf_op jit(solution)/shard_map/ppermute | solution.py:320
  92.6 20.7 %collective-permute-start = (s32[16]{0:T(128)S(1)}, s32[16]{0:T(128)S(1)}, u32[]{:S(2)}, u32[]{:S(2)}) collective-permute-start(s32[16]{0:T(128)S(1)} %copy-done.5), channel_id=1, source_target_pairs={{0,4},{12,8},{1,5},{13,9},{2,6},{14,10},{3,7},{15,11},{16,20},{28,... | collective-permute-start | bytes 200 | tf_op jit(solution)/shard_map/ppermute | solution.py:320
  109.6 3.7 %copy-start.15 = (s32[16]{0:T(128)S(1)}, s32[16]{0:T(128)}, u32[]{:S(2)}) copy-start(s32[16]{0:T(128)} %refs_2_.13) | copy-start | bytes 196
  109.6 20.2 %copy-start.11 = (bf16[8,32,1280]{2,1,0:T(8,128)(2,1)S(1)}, bf16[8,32,1280]{2,1,0:T(8,128)(2,1)}, u32[]{:S(2)}) copy-start(bf16[8,32,1280]{2,1,0:T(8,128)(2,1)} %get-tuple-element.17) | copy-start | bytes 1966084
  109.6 24.4 %collective-permute-start.3 = (bf16[8,32,1280]{2,1,0:T(8,128)(2,1)S(1)}, bf16[8,32,1280]{2,1,0:T(8,128)(2,1)S(1)}, u32[]{:S(2)}, u32[]{:S(2)}) collective-permute-start(bf16[8,32,1280]{2,1,0:T(8,128)(2,1)S(1)} %copy-done.12), channel_id=1, source_target_pairs={{0,4},{12,8},{1,5},{13,9},{2,6},{14,10},{3,7},{15,11},{16,20},{28,... | collective-permute-start | bytes 1966088 | tf_op jit(solution)/shard_map/ppermute | solution.py:320
  111.1 1.0 copy-start.10
  111.1 34.9 %collective-permute-start.13 = (bf16[2048,256]{1,0:T(8,128)(2,1)}, bf16[2048,256]{1,0:T(8,128)(2,1)S(1)}, u32[]{:S(2)}, u32[]{:S(2)}) collective-permute-start(bf16[2048,256]{1,0:T(8,128)(2,1)} %collective-permute-done.2.refs_5_), channel_id=1, source_target_pairs={{4,8},{8,4},{5,9},{9,5},{6,10},{10,6},{7,11},{11,7},{20,24},{24,20... | collective-permute-start | bytes 3145736 | tf_op jit(solution)/shard_map/ppermute | solution.py:320
  113.3 23.0 %copy-start.16 = (s32[16]{0:T(128)}, s32[16]{0:T(128)S(1)}, u32[]{:S(2)}) copy-start(s32[16]{0:T(128)S(1)} %collective-permute-done.refs_3_) | copy-start | bytes 196
  113.3 16.5 %collective-permute-start.1 = (s32[16]{0:T(128)S(1)}, s32[16]{0:T(128)S(1)}, u32[]{:S(2)}, u32[]{:S(2)}) collective-permute-start(s32[16]{0:T(128)S(1)} %copy-done.15), channel_id=1, source_target_pairs={{0,4},{12,8},{1,5},{13,9},{2,6},{14,10},{3,7},{15,11},{16,20},{28,... | collective-permute-start | bytes 200 | tf_op jit(solution)/shard_map/ppermute | solution.py:320
  129.8 6.5 %copy-start.17 = (s32[16]{0:T(128)}, s32[16]{0:T(128)S(1)}, u32[]{:S(2)}) copy-start(s32[16]{0:T(128)S(1)} %collective-permute-done.1.refs_4_) | copy-start | bytes 196
  129.8 16.1 %collective-permute-start.12 = (bf16[8,32,1280]{2,1,0:T(8,128)(2,1)S(1)}, bf16[8,32,1280]{2,1,0:T(8,128)(2,1)S(1)}, u32[]{:S(2)}, u32[]{:S(2)}) collective-permute-start(bf16[8,32,1280]{2,1,0:T(8,128)(2,1)S(1)} %copy-done.11), channel_id=1, source_target_pairs={{0,4},{12,8},{1,5},{13,9},{2,6},{14,10},{3,7},{15,11},{16,20},{28,... | collective-permute-start | bytes 1966088 | tf_op jit(solution)/shard_map/ppermute | solution.py:320
  134.0 2.3 %copy-start.13 = (bf16[8,32,1280]{2,1,0:T(8,128)(2,1)}, bf16[8,32,1280]{2,1,0:T(8,128)(2,1)S(1)}, u32[]{:S(2)}) copy-start(bf16[8,32,1280]{2,1,0:T(8,128)(2,1)S(1)} %collective-permute-done.3.refs_5_) | copy-start | bytes 1966084
  134.0 24.8 %collective-permute-start.15 = (bf16[2048,256]{1,0:T(8,128)(2,1)}, bf16[2048,256]{1,0:T(8,128)(2,1)S(1)}, u32[]{:S(2)}, u32[]{:S(2)}) collective-permute-start(bf16[2048,256]{1,0:T(8,128)(2,1)} %collective-permute-done.8.refs_6_), channel_id=1, source_target_pairs={{4,0},{8,12},{5,1},{9,13},{6,2},{10,14},{7,3},{11,15},{20,16},{24,... | collective-permute-start | bytes 3145736 | tf_op jit(solution)/shard_map/ppermute | solution.py:320
  135.3 1.2 copy-start.7
  135.4 1.5 copy-start.8
  146.0 1.0 copy-start.14
  146.0 1.4 copy-start.6
  147.3 2.4 %copy-start.2 = (bf16[8,32,1024]{2,1,0:T(8,128)(2,1)S(1)}, bf16[8,32,1024]{2,1,0:T(8,128)(2,1)}, u32[]{:S(2)}) copy-start(bf16[8,32,1024]{2,1,0:T(8,128)(2,1)} %get-tuple-element.15) | copy-start | bytes 1572868
  148.4 32.6 %collective-permute-start.14 = (bf16[8,32,1024]{2,1,0:T(8,128)(2,1)}, bf16[8,32,1024]{2,1,0:T(8,128)(2,1)S(1)}, u32[]{:S(2)}, u32[]{:S(2)}) collective-permute-start(bf16[8,32,1024]{2,1,0:T(8,128)(2,1)} %get-tuple-element.19), channel_id=1, source_target_pairs={{4,0},{8,12},{5,1},{9,13},{6,2},{10,14},{7,3},{11,15},{20,16},{24,... | collective-permute-start | bytes 1572872 | tf_op jit(solution)/shard_map/ppermute | solution.py:320
  149.7 39.1 %collective-permute-start.11 = (bf16[8,32,1024]{2,1,0:T(8,128)(2,1)S(1)}, bf16[8,32,1024]{2,1,0:T(8,128)(2,1)S(1)}, u32[]{:S(2)}, u32[]{:S(2)}) collective-permute-start(bf16[8,32,1024]{2,1,0:T(8,128)(2,1)S(1)} %copy-done.2), channel_id=1, source_target_pairs={{4,0},{8,12},{5,1},{9,13},{6,2},{10,14},{7,3},{11,15},{20,16},{24,... | collective-permute-start | bytes 1572872 | tf_op jit(solution)/shard_map/ppermute | solution.py:320
  158.8 1.0 copy-start.9
  181.0 7.8 %copy-start.3 = (bf16[8,32,1024]{2,1,0:T(8,128)(2,1)}, bf16[8,32,1024]{2,1,0:T(8,128)(2,1)S(1)}, u32[]{:S(2)}) copy-start(bf16[8,32,1024]{2,1,0:T(8,128)(2,1)S(1)} %collective-permute-done.14.got1) | copy-start | bytes 1572868
  188.8 0.8 copy-start.4
